TPU v7x, 256 devices: a whole 4x4x8 slice. The times are simulated.
256 devices in a mesh: leaf: 32 (over x, z), fac: 8 (over y, core).
Axes of the slice: x: 4, y: 4, z: 8, core: 2. Of those that a mesh axis runs over, the one named last changes fastest.
Arguments:
- loads: bfloat16 [256, 131072], P(None, ('leaf', 'fac')), may hold values from -6 to 6
- leaf_sizes: int32 [32], P('leaf'), may hold values from 2048 to 4096, as said below
- tree_order: int32 [32, 4096], P('leaf'), may hold values from 0 to 4095, each once within a row
- leaf_inverse: bfloat16 [131072, 4096], P(('leaf', 'fac')), may hold values from -0.09375 to 0.09375
- left_factors: bfloat16 [3, 131072, 128], P(None, ('leaf', 'fac')), may hold values from -0.5 to 0.5
- right_factors: bfloat16 [3, 131072, 128], P(None, ('leaf', 'fac')), may hold values from -0.0234375 to 0.0234375
Outputs:
- solution: float32 [256, 131072], P(None, ('leaf', 'fac'))
Inputs may be any that keep to these rules, and one draw needn't show every extreme that they name: `leaf_sizes`: some leaf cluster is full in every draw. `tree_order`: each row is a permutation of the cluster's slots.
All inputs are finite; a program needn't handle non-finite values.
Results may differ from a plain program's by a relative error of at most 0.0003.
Values may be sent and summed in bfloat16 or wider, within the bound.
A program may use at most 64 MiB of HBM per device.

v0:
```python
import jax
import jax.numpy as jnp
from jax import lax
from jax.sharding import PartitionSpec as P


def from_partner(array, axis, distance):
    return lax.ppermute(array, axis, [(i, i ^ 1 << distance) for i in range(lax.axis_size(axis))])


def sibling_sum(partial_value, bit):
    for lower in range(bit):
        partial_value = partial_value + from_partner(partial_value, "leaf", lower)
    return from_partner(partial_value, "leaf", bit)


def body(loads, leaf_sizes, tree_order, leaf_inverse, left_factors, right_factors):
    rows = loads.shape[1]
    whole = lax.all_gather(loads, "fac", axis=1, tiled=True)
    leaf_width = whole.shape[1]
    position = jnp.arange(leaf_width, dtype=jnp.int32)
    ordered = jnp.take(whole, tree_order[0], axis=1)
    ordered = jnp.where((position < leaf_sizes[0])[None, :], ordered, jnp.zeros_like(ordered))
    field = lax.dot_general(
        ordered, leaf_inverse, (((1,), (1,)), ((), ())), preferred_element_type=jnp.float32
    )
    first_row = lax.axis_index("fac") * rows
    live = first_row + jnp.arange(rows, dtype=jnp.int32) < leaf_sizes[0]
    field = jnp.where(live[None, :], field, 0.0)
    bits = lax.axis_size("leaf").bit_length() - 1
    levels = left_factors.shape[0]
    for level in range(levels):
        bit = bits - levels + level
        right_block = right_factors[level].astype(jnp.float32)
        left_block = left_factors[level].astype(jnp.float32)
        coef = jnp.dot(field, right_block, precision=lax.Precision.HIGHEST)
        coef = lax.psum(coef, "fac")
        partner = sibling_sum(coef, bit)
        update = lax.dot_general(
            partner, left_block, (((1,), (1,)), ((), ())), precision=lax.Precision.HIGHEST
        )
        field = jnp.where(live[None, :], field + update, 0.0)
    return field


def solution(mesh):
    placed = (
        P(None, ("leaf", "fac")),
        P("leaf"),
        P("leaf", None),
        P(("leaf", "fac"), None),
        P(None, ("leaf", "fac"), None),
        P(None, ("leaf", "fac"), None),
    )
    return jax.shard_map(
        body, mesh=mesh, in_specs=placed, out_specs=P(None, ("leaf", "fac")), check_vma=False
    )
```

profile of v0, /device:TPU:28, one launch (start us, length us, event | category | flops | bytes accessed | tf_op | source)
XLA Modules:
  0.0 358.0 jit_solution(9875573531698220922)
XLA Ops:
  10.6 28.1 %all-gather.2.cloned.1.call-done = bf16[256,4096]{0,1:T(8,128)(2,1)} async-done(((bf16[256,512]{0,1:T(8,128)(2,1)}), bf16[256,4096]{0,1:T(8,128)(2,1)}) %all-gather.2.cloned.1.call-update) | async-done | bytes 2097168 | tf_op jit(solution)/shard_map/all_gather | solution.py:19
  38.6 14.9 %gather_fusion = bf16[4096,256]{1,0:T(8,128)(2,1)S(1)} fusion(bf16[256,4096]{0,1:T(8,128)(2,1)} %all-gather.2.cloned.1.call-done, s32[4096]{0:T(1024)S(1)} %broadcast_clamp_fusion), kind=kCustom, calls=%fused_computation | custom fusion | bytes 4210688 | tf_op jit(solution)/shard_map/jit(_take)/gather | solution.py:22
  53.5 5.1 %fusion.8 = f32[256,512]{1,0:T(8,128)S(1)} fusion(bf16[512,4096]{1,0:T(8,128)(2,1)} %param.9, bf16[4096,256]{1,0:T(8,128)(2,1)S(1)} %gather_fusion, pred[4096]{0:T(1024)(128)(4,1)S(1)} %get-tuple-element.5, pred[4096]{0:T(1024)(128)(4,1)S(1)} %get-tuple-element.6, pred[512]{0:T(512)(128)(4,1)S(1)} %add_compare_fusion), kind=kOutput, calls=%fused_computation.12 | convolution fusion | flops 1075970048 | bytes 6824448 | tf_op jit(solution)/shard_map/dot_general | solution.py:24
  59.7 63.6 %all-reduce.4.cloned.1.call-done = f32[256,128]{1,0:T(8,128)} async-done(((f32[256,128]{1,0:T(8,128)}), f32[256,128]{1,0:T(8,128)}) %all-reduce.4.cloned.1.call-update) | async-done | bytes 131088 | tf_op jit(solution)/shard_map/psum | solution.py:37
  124.9 4.7 %collective-permute-done = f32[256,128]{1,0:T(8,128)S(1)} collective-permute-done((f32[256,128]{1,0:T(8,128)}, f32[256,128]{1,0:T(8,128)S(1)}, u32[]{:S(2)}, u32[]{:S(2)}) %collective-permute-start) | collective-permute-done | bytes 131104 | tf_op jit(solution)/shard_map/ppermute | solution.py:8
  130.5 2.6 collective-permute-start.1
  133.1 6.4 %collective-permute-done.1 = f32[256,128]{1,0:T(8,128)S(1)} collective-permute-done((f32[256,128]{1,0:T(8,128)S(1)}, f32[256,128]{1,0:T(8,128)S(1)}, u32[]{:S(2)}, u32[]{:S(2)}) %collective-permute-start.1) | collective-permute-done | bytes 131104 | tf_op jit(solution)/shard_map/ppermute | solution.py:8
  139.5 5.8 %collective-permute-start.2 = (f32[256,128]{1,0:T(8,128)S(1)}, f32[256,128]{1,0:T(8,128)S(1)}, u32[]{:S(2)}, u32[]{:S(2)}) collective-permute-start(f32[256,128]{1,0:T(8,128)S(1)} %add.80), channel_id=1, source_target_pairs={{0,32},{8,40},{16,48},{24,56},{32,0},{40,8},{48,16},{56,24},{64,96... | collective-permute-start | bytes 393224 | tf_op jit(solution)/shard_map/ppermute | solution.py:8
  145.3 6.4 %collective-permute-done.2 = f32[256,128]{1,0:T(8,128)S(1)} collective-permute-done((f32[256,128]{1,0:T(8,128)S(1)}, f32[256,128]{1,0:T(8,128)S(1)}, u32[]{:S(2)}, u32[]{:S(2)}) %collective-permute-start.2) | collective-permute-done | bytes 131104 | tf_op jit(solution)/shard_map/ppermute | solution.py:8
  153.2 60.4 %all-reduce.6.cloned.1.call-done = f32[256,128]{1,0:T(8,128)} async-done(((f32[256,128]{1,0:T(8,128)}), f32[256,128]{1,0:T(8,128)}) %all-reduce.6.cloned.1.call-update) | async-done | bytes 131088 | tf_op jit(solution)/shard_map/psum | solution.py:37
  215.2 4.7 %collective-permute-done.3 = f32[256,128]{1,0:T(8,128)S(1)} collective-permute-done((f32[256,128]{1,0:T(8,128)}, f32[256,128]{1,0:T(8,128)S(1)}, u32[]{:S(2)}, u32[]{:S(2)}) %collective-permute-start.3) | collective-permute-done | bytes 131104 | tf_op jit(solution)/shard_map/ppermute | solution.py:8
  220.8 2.6 collective-permute-start.4
  223.4 6.4 %collective-permute-done.4 = f32[256,128]{1,0:T(8,128)S(1)} collective-permute-done((f32[256,128]{1,0:T(8,128)S(1)}, f32[256,128]{1,0:T(8,128)S(1)}, u32[]{:S(2)}, u32[]{:S(2)}) %collective-permute-start.4) | collective-permute-done | bytes 131104 | tf_op jit(solution)/shard_map/ppermute | solution.py:8
  229.8 5.8 %collective-permute-start.5 = (f32[256,128]{1,0:T(8,128)S(1)}, f32[256,128]{1,0:T(8,128)S(1)}, u32[]{:S(2)}, u32[]{:S(2)}) collective-permute-start(f32[256,128]{1,0:T(8,128)S(1)} %add.83), channel_id=1, source_target_pairs={{0,32},{8,40},{16,48},{24,56},{32,0},{40,8},{48,16},{56,24},{64,96... | collective-permute-start | bytes 393224 | tf_op jit(solution)/shard_map/ppermute | solution.py:8
  235.6 6.4 %collective-permute-done.5 = f32[256,128]{1,0:T(8,128)S(1)} collective-permute-done((f32[256,128]{1,0:T(8,128)S(1)}, f32[256,128]{1,0:T(8,128)S(1)}, u32[]{:S(2)}, u32[]{:S(2)}) %collective-permute-start.5) | collective-permute-done | bytes 131104 | tf_op jit(solution)/shard_map/ppermute | solution.py:8
  243.3 3.8 %collective-permute-done.6 = f32[256,128]{1,0:T(8,128)S(1)} collective-permute-done((f32[256,128]{1,0:T(8,128)S(1)}, f32[256,128]{1,0:T(8,128)S(1)}, u32[]{:S(2)}, u32[]{:S(2)}) %collective-permute-start.6) | collective-permute-done | bytes 131104 | tf_op jit(solution)/shard_map/ppermute | solution.py:8
  248.5 60.4 %all-reduce.8.cloned.1.call-done = f32[256,128]{1,0:T(8,128)} async-done(((f32[256,128]{1,0:T(8,128)}), f32[256,128]{1,0:T(8,128)}) %all-reduce.8.cloned.1.call-update) | async-done | bytes 131088 | tf_op jit(solution)/shard_map/psum | solution.py:37
  310.5 4.7 %collective-permute-done.7 = f32[256,128]{1,0:T(8,128)S(1)} collective-permute-done((f32[256,128]{1,0:T(8,128)}, f32[256,128]{1,0:T(8,128)S(1)}, u32[]{:S(2)}, u32[]{:S(2)}) %collective-permute-start.7) | collective-permute-done | bytes 131104 | tf_op jit(solution)/shard_map/ppermute | solution.py:8
  316.1 2.6 collective-permute-start.8
  318.8 6.4 %collective-permute-done.8 = f32[256,128]{1,0:T(8,128)S(1)} collective-permute-done((f32[256,128]{1,0:T(8,128)S(1)}, f32[256,128]{1,0:T(8,128)S(1)}, u32[]{:S(2)}, u32[]{:S(2)}) %collective-permute-start.8) | collective-permute-done | bytes 131104 | tf_op jit(solution)/shard_map/ppermute | solution.py:8
  325.1 5.8 %collective-permute-start.9 = (f32[256,128]{1,0:T(8,128)S(1)}, f32[256,128]{1,0:T(8,128)S(1)}, u32[]{:S(2)}, u32[]{:S(2)}) collective-permute-start(f32[256,128]{1,0:T(8,128)S(1)} %add.87), channel_id=1, source_target_pairs={{0,32},{8,40},{16,48},{24,56},{32,0},{40,8},{48,16},{56,24},{64,96... | collective-permute-start | bytes 393224 | tf_op jit(solution)/shard_map/ppermute | solution.py:8
  331.0 6.4 %collective-permute-done.9 = f32[256,128]{1,0:T(8,128)S(1)} collective-permute-done((f32[256,128]{1,0:T(8,128)S(1)}, f32[256,128]{1,0:T(8,128)S(1)}, u32[]{:S(2)}, u32[]{:S(2)}) %collective-permute-start.9) | collective-permute-done | bytes 131104 | tf_op jit(solution)/shard_map/ppermute | solution.py:8
  338.6 5.1 %collective-permute-done.10 = f32[256,128]{1,0:T(8,128)S(1)} collective-permute-done((f32[256,128]{1,0:T(8,128)S(1)}, f32[256,128]{1,0:T(8,128)S(1)}, u32[]{:S(2)}, u32[]{:S(2)}) %collective-permute-start.10) | collective-permute-done | bytes 131104 | tf_op jit(solution)/shard_map/ppermute | solution.py:8
  343.9 6.5 %collective-permute-done.11 = f32[256,128]{1,0:T(8,128)S(1)} collective-permute-done((f32[256,128]{1,0:T(8,128)S(1)}, f32[256,128]{1,0:T(8,128)S(1)}, u32[]{:S(2)}, u32[]{:S(2)}) %collective-permute-start.11) | collective-permute-done | bytes 131104 | tf_op jit(solution)/shard_map/ppermute | solution.py:8
  (38 shorter events, 18.7 us)
Async XLA Ops:
  6.5 32.1 %all-gather.2.cloned.1.call-start = ((), (), s32[]{:S(2)}) async-start(), calls=%async_computation | async-start | bytes 2359296 | tf_op jit(solution)/shard_map/all_gather | solution.py:19
  8.4 115.0 %all-reduce.4.cloned.1.call-start = ((), (), s32[]{:S(2)}) async-start(), calls=%async_computation.1 | async-start | bytes 262144 | tf_op jit(solution)/shard_map/psum | solution.py:37
  53.5 5.1 %copy-start.1 = (bf16[3,512,128]{2,1,0:T(8,128)(2,1)S(1)}, bf16[3,512,128]{2,1,0:T(8,128)(2,1)}, u32[]{:S(2)}) copy-start(bf16[3,512,128]{2,1,0:T(8,128)(2,1)} %param.11) | copy-start | bytes 1179652
  53.5 98.2 %copy-start = (bf16[3,512,128]{2,1,0:T(8,128)(2,1)S(1)}, bf16[3,512,128]{2,1,0:T(8,128)(2,1)}, u32[]{:S(2)}) copy-start(bf16[3,512,128]{2,1,0:T(8,128)(2,1)} %param.10) | copy-start | bytes 1179652
  59.7 154.0 %all-reduce.6.cloned.1.call-start = ((), (), s32[]{:S(2)}) async-start(), calls=%async_computation.2 | async-start | bytes 262144 | tf_op jit(solution)/shard_map/psum | solution.py:37
  123.3 6.3 %collective-permute-start = (f32[256,128]{1,0:T(8,128)}, f32[256,128]{1,0:T(8,128)S(1)}, u32[]{:S(2)}, u32[]{:S(2)}) collective-permute-start(f32[256,128]{1,0:T(8,128)} %all-reduce.4.cloned.1.call-done), channel_id=1, source_target_pairs={{0,8},{8,0},{16,24},{24,16},{32,40},{40,32},{48,56},{56,48},{64,72... | collective-permute-start | bytes 393224 | tf_op jit(solution)/shard_map/ppermute | solution.py:8
  130.5 9.0 %collective-permute-start.1 = (f32[256,128]{1,0:T(8,128)S(1)}, f32[256,128]{1,0:T(8,128)S(1)}, u32[]{:S(2)}, u32[]{:S(2)}) collective-permute-start(f32[256,128]{1,0:T(8,128)S(1)} %add.79), channel_id=1, source_target_pairs={{0,16},{8,24},{16,0},{24,8},{32,48},{40,56},{48,32},{56,40},{64,80... | collective-permute-start | bytes 393224 | tf_op jit(solution)/shard_map/ppermute | solution.py:8
  139.5 12.2 %collective-permute-start.2 = (f32[256,128]{1,0:T(8,128)S(1)}, f32[256,128]{1,0:T(8,128)S(1)}, u32[]{:S(2)}, u32[]{:S(2)}) collective-permute-start(f32[256,128]{1,0:T(8,128)S(1)} %add.80), channel_id=1, source_target_pairs={{0,32},{8,40},{16,48},{24,56},{32,0},{40,8},{48,16},{56,24},{64,96... | collective-permute-start | bytes 393224 | tf_op jit(solution)/shard_map/ppermute | solution.py:8
  153.2 155.8 %all-reduce.8.cloned.1.call-start = ((), (), s32[]{:S(2)}) async-start(), calls=%async_computation.3 | async-start | bytes 262144 | tf_op jit(solution)/shard_map/psum | solution.py:37
  213.6 6.3 %collective-permute-start.3 = (f32[256,128]{1,0:T(8,128)}, f32[256,128]{1,0:T(8,128)S(1)}, u32[]{:S(2)}, u32[]{:S(2)}) collective-permute-start(f32[256,128]{1,0:T(8,128)} %all-reduce.6.cloned.1.call-done), channel_id=1, source_target_pairs={{0,8},{8,0},{16,24},{24,16},{32,40},{40,32},{48,56},{56,48},{64,72... | collective-permute-start | bytes 393224 | tf_op jit(solution)/shard_map/ppermute | solution.py:8
  220.8 9.0 %collective-permute-start.4 = (f32[256,128]{1,0:T(8,128)S(1)}, f32[256,128]{1,0:T(8,128)S(1)}, u32[]{:S(2)}, u32[]{:S(2)}) collective-permute-start(f32[256,128]{1,0:T(8,128)S(1)} %add.82), channel_id=1, source_target_pairs={{0,16},{8,24},{16,0},{24,8},{32,48},{40,56},{48,32},{56,40},{64,80... | collective-permute-start | bytes 393224 | tf_op jit(solution)/shard_map/ppermute | solution.py:8
  229.8 12.2 %collective-permute-start.5 = (f32[256,128]{1,0:T(8,128)S(1)}, f32[256,128]{1,0:T(8,128)S(1)}, u32[]{:S(2)}, u32[]{:S(2)}) collective-permute-start(f32[256,128]{1,0:T(8,128)S(1)} %add.83), channel_id=1, source_target_pairs={{0,32},{8,40},{16,48},{24,56},{32,0},{40,8},{48,16},{56,24},{64,96... | collective-permute-start | bytes 393224 | tf_op jit(solution)/shard_map/ppermute | solution.py:8
  242.0 5.1 %collective-permute-start.6 = (f32[256,128]{1,0:T(8,128)S(1)}, f32[256,128]{1,0:T(8,128)S(1)}, u32[]{:S(2)}, u32[]{:S(2)}) collective-permute-start(f32[256,128]{1,0:T(8,128)S(1)} %add.84), channel_id=1, source_target_pairs={{0,64},{8,72},{16,80},{24,88},{32,96},{40,104},{48,112},{56,120},{... | collective-permute-start | bytes 393224 | tf_op jit(solution)/shard_map/ppermute | solution.py:8
  309.0 6.3 %collective-permute-start.7 = (f32[256,128]{1,0:T(8,128)}, f32[256,128]{1,0:T(8,128)S(1)}, u32[]{:S(2)}, u32[]{:S(2)}) collective-permute-start(f32[256,128]{1,0:T(8,128)} %all-reduce.8.cloned.1.call-done), channel_id=1, source_target_pairs={{0,8},{8,0},{16,24},{24,16},{32,40},{40,32},{48,56},{56,48},{64,72... | collective-permute-start | bytes 393224 | tf_op jit(solution)/shard_map/ppermute | solution.py:8
  316.1 9.0 %collective-permute-start.8 = (f32[256,128]{1,0:T(8,128)S(1)}, f32[256,128]{1,0:T(8,128)S(1)}, u32[]{:S(2)}, u32[]{:S(2)}) collective-permute-start(f32[256,128]{1,0:T(8,128)S(1)} %add.86), channel_id=1, source_target_pairs={{0,16},{8,24},{16,0},{24,8},{32,48},{40,56},{48,32},{56,40},{64,80... | collective-permute-start | bytes 393224 | tf_op jit(solution)/shard_map/ppermute | solution.py:8
  325.1 12.2 %collective-permute-start.9 = (f32[256,128]{1,0:T(8,128)S(1)}, f32[256,128]{1,0:T(8,128)S(1)}, u32[]{:S(2)}, u32[]{:S(2)}) collective-permute-start(f32[256,128]{1,0:T(8,128)S(1)} %add.87), channel_id=1, source_target_pairs={{0,32},{8,40},{16,48},{24,56},{32,0},{40,8},{48,16},{56,24},{64,96... | collective-permute-start | bytes 393224 | tf_op jit(solution)/shard_map/ppermute | solution.py:8
  337.4 6.4 %collective-permute-start.10 = (f32[256,128]{1,0:T(8,128)S(1)}, f32[256,128]{1,0:T(8,128)S(1)}, u32[]{:S(2)}, u32[]{:S(2)}) collective-permute-start(f32[256,128]{1,0:T(8,128)S(1)} %add.88), channel_id=1, source_target_pairs={{0,64},{8,72},{16,80},{24,88},{32,96},{40,104},{48,112},{56,120},{... | collective-permute-start | bytes 393224 | tf_op jit(solution)/shard_map/ppermute | solution.py:8
  343.8 6.6 %collective-permute-start.11 = (f32[256,128]{1,0:T(8,128)S(1)}, f32[256,128]{1,0:T(8,128)S(1)}, u32[]{:S(2)}, u32[]{:S(2)}) collective-permute-start(f32[256,128]{1,0:T(8,128)S(1)} %add.89), channel_id=1, source_target_pairs={{0,128},{8,136},{16,144},{24,152},{32,160},{40,168},{48,176},{56,1... | collective-permute-start | bytes 393224 | tf_op jit(solution)/shard_map/ppermute | solution.py:8
Sparse Core Ops, SparseCore 0:
  9.2 29.3 all-gather.1
  59.8 63.5 all-reduce.3
  153.3 60.2 all-reduce.5
  248.7 60.2 all-reduce.7
where the time goes:
time: 358 us
  waiting for transfers between devices  280 us (78%)
  starting transfers between devices  32.8 us (9%)
  local copies, waits for them, and re-layouts  16.7 us (5%)
  between operations  13.9 us (4%)
  matrix products  10.1 us (3%)
  other arithmetic  4.34 us (1%)
    psum x3, waiting for transfers between devices, body(): coef = lax.psum(coef, 'fac')  184 us
    ppermute x12, waiting for transfers between devices, from_partner(): lax.ppermute(array, axis, [(i, i ^ 1 << distance) for i in range(lax.axis...  67.7 us
    ppermute x12, starting transfers between devices, from_partner(): lax.ppermute(array, axis, [(i, i ^ 1 << distance) for i in range(lax.axis...  32.6 us
    all_gather x1, waiting for transfers between devices, body(): whole = lax.all_gather(loads, 'fac', axis=1, tiled=True)  28.1 us
    gather x1, local copies, waits for them, and re-layouts, body(): ordered = jnp.take(whole, tree_order[0], axis=1)  14.9 us
  transfers between devices with their start and end apart: 16, of which 16 were waited for; matrix products, arithmetic and copies ran while one was open for 0% of the time, Pallas kernels for 0%

commit v1 on v0

v1 whole, which is shorter than its diff:
```python
import functools

import jax
import jax.numpy as jnp
from jax import lax
from jax.experimental import pallas as pl
from jax.experimental.pallas import tpu as pltpu
from jax.sharding import PartitionSpec as P

CASES = 256
RANK = 128
LEVELS = 3
SLOTS = 4096
ROWS = 512
HALF = 256
WIDE = LEVELS * RANK
COPIES = 64
MESH = pl.DeviceIdType.MESH


def kernel(
    loads_ref, size_ref, order_ref, inverse_ref, left_ref, right_ref, out_ref,
    raw, blocks, order, match, ordered, inverse, left, right, left_t, right_w,
    field, coef, coef_core, coef_y, coef_mine, in_core, in_y, in_z, sent, in_node, partner,
    mix, mix_core, mix_half, mix_near, mix_far, mix_z, mix_y, mixing,
    local_sem, send_sem, recv_sem,
):
    leaf, fac = lax.axis_index("leaf"), lax.axis_index("fac")
    x, z = lax.div(leaf, 8), lax.rem(leaf, 8)
    y, core = lax.div(fac, 2), lax.rem(fac, 2)
    z_hi, z_lo = lax.div(z, 4), lax.rem(z, 4)
    x_pair = x + 1 - 2 * lax.rem(x, 2)
    x_far = [lax.rem(x + 2, 4), 3 - x]

    def at(x_=x, z_=z, y_=y, core_=core):
        return (x_ * 8 + z_, y_ * 2 + core_)

    def y_off(o):
        return lax.rem(y + o, 4)

    def z_off(o, flip=0):
        return lax.rem(z_hi + flip, 2) * 4 + lax.rem(z_lo + o, 4)

    sibling = at(core_=1 - core)
    near_z = [z_off(o) for o in (1, 2, 3)]
    flip_z = [z_off(o, 1) for o in range(4)]
    z_all = [z_off(o, f) for f in range(2) for o in range(4)]
    partners = [sibling]
    partners += [at(y_=y_off(o)) for o in (1, 2, 3)]
    partners += [at(z_=other) for other in near_z + flip_z]
    partners += [at(z_=other, core_=1 - core) for other in near_z]
    partners += [at(x_=x_pair, z_=other) for other in z_all]
    partners += [at(x_=far, z_=z_off(0, f)) for far in x_far for f in range(2)]

    barrier = pltpu.get_barrier_semaphore()
    for other in partners:
        pl.semaphore_signal(barrier, inc=1, device_id=other, device_id_type=MESH)

    copies = []

    def send(src, dst, target):
        i = len(copies)
        copy = pltpu.make_async_remote_copy(
            src_ref=src, dst_ref=dst, send_sem=send_sem.at[i], recv_sem=recv_sem.at[i],
            device_id=target, device_id_type=MESH,
        )
        copies.append(copy)
        copy.start()
        return copy

    def fetch(i, src, dst):
        copy = pltpu.make_async_copy(src, dst, local_sem.at[i])
        copy.start()
        return copy

    got_loads = fetch(0, loads_ref, raw)
    got_order = fetch(1, order_ref, order)
    got_left = fetch(2, left_ref, left)
    got_right = fetch(3, right_ref, right)
    got_inverse = fetch(4, inverse_ref, inverse)

    got_loads.wait()
    blocks[fac] = raw[...].T
    pl.semaphore_wait(barrier, len(partners))

    def half(block, h):
        return blocks.at[block, pl.ds(h * HALF, HALF), :]

    def pass_on(block, h, target):
        return send(half(block, h), half(block, h), target)

    def block_of(y_, core_=core):
        return y_ * 2 + core_

    up, down = y_off(1), y_off(3)
    up_first = pass_on(fac, 0, at(y_=up))
    down_first = pass_on(fac, 1, at(y_=down))
    own_sib = send(blocks.at[fac], blocks.at[fac], sibling)
    up_second = pass_on(fac, 1, at(y_=up))
    down_second = pass_on(fac, 0, at(y_=down))

    size = size_ref[0]
    got_order.wait()

    @pl.loop(0, 32)
    def _(r):
        place = r * 128 + lax.broadcasted_iota(jnp.int32, (1, 128), 1)
        row = jnp.where(place < size, order[pl.ds(r, 1), :], -1)
        match[pl.ds(pl.multiple_of(r * 128, 128), 128), :] = jnp.broadcast_to(row, (128, 128)).T

    first_row = fac * ROWS

    def permute(parts, first=False):
        @pl.loop(0, 2)
        def _(m):
            rows = pl.ds(pl.multiple_of(m * 2048, 2048), 2048)
            slot = match[rows, :]
            total = None
            for block, start, count in parts:
                picks = []
                for j in range(count // 128):
                    here = block * ROWS + start + j * 128
                    column = here + lax.broadcasted_iota(jnp.int32, (2048, 128), 1)
                    picks.append(jnp.where(slot == column, 1.0, 0.0).astype(jnp.bfloat16))
                term = jnp.dot(
                    jnp.concatenate(picks, axis=1), blocks[block, pl.ds(start, count), :],
                    preferred_element_type=jnp.float32,
                )
                total = term if total is None else total + term
            total = total.astype(jnp.bfloat16)
            if first:
                ordered[rows, :] = total
            else:
                ordered[rows, :] += total

    got_left.wait()
    got_right.wait()
    for level in range(LEVELS):
        live = first_row + lax.broadcasted_iota(jnp.int32, (RANK, ROWS), 1) < size
        turned = left[level].T
        left_t[level * RANK:(level + 1) * RANK, :] = jnp.where(live, turned, jnp.zeros_like(turned))
        right_w[:, level * RANK:(level + 1) * RANK] = right[level]
    mix[:, :2 * RANK] = jnp.dot(left_t[:RANK, :], right_w[:, RANK:], preferred_element_type=jnp.float32)
    mix[:, 2 * RANK:] = jnp.dot(left_t[RANK:2 * RANK, :], right_w[:, 2 * RANK:], preferred_element_type=jnp.float32)
    mix_sib = send(mix.at[pl.ds(pl.multiple_of(64 * (1 - core), 64), 64), :], mix_core, sibling)

    permute([(fac, 0, ROWS)], first=True)

    mix_sib.wait_recv()
    mix_half[...] = mix[pl.ds(pl.multiple_of(64 * core, 64), 64), :] + mix_core[...]
    to_z = []
    for o in range(4):
        rows = pl.ds(pl.multiple_of(16 * lax.rem(z_lo + o, 4), 16), 16)
        to_z.append(send(mix_half.at[rows, pl.ds(0, 2 * RANK)], mix_near.at[o], at(z_=z_off(o, 1))))
        for f in range(2):
            to_z.append(send(
                mix_half.at[rows, pl.ds(2 * RANK, RANK)], mix_far.at[f * 4 + o],
                at(x_=x_pair, z_=z_off(o, f)),
            ))

    own_sib.wait_recv()
    other = block_of(y, 1 - core)
    permute([(other, 0, ROWS)])

    def stage(from_down, h_down, from_up, h_up, block_down, block_up):
        from_down.wait_recv()
        relay_down = pass_on(block_down, h_down, sibling)
        from_up.wait_recv()
        relay_up = pass_on(block_up, h_up, sibling)
        return relay_down, relay_up

    below, above, across = y_off(3), y_off(1), y_off(2)
    up_first.wait_recv()
    relay_a = pass_on(block_of(below), 0, sibling)
    forward_up = pass_on(block_of(below), 0, at(y_=up))
    down_first.wait_recv()
    relay_b = pass_on(block_of(above), 1, sibling)
    forward_down = pass_on(block_of(above), 1, at(y_=down))
    permute([(block_of(below), 0, HALF), (block_of(above), HALF, HALF)])
    relay_a.wait_recv()
    relay_b.wait_recv()
    permute([(block_of(below, 1 - core), 0, HALF), (block_of(above, 1 - core), HALF, HALF)])

    for copy in to_z:
        copy.wait_recv()
    mix_z[:, :2 * RANK] = mix_near[0] + mix_near[1] + mix_near[2] + mix_near[3]
    far = mix_far[0]
    for j in range(1, 8):
        far = far + mix_far[j]
    mix_z[:, 2 * RANK:] = far

    relay_a, relay_b = stage(up_second, 1, down_second, 0, block_of(below), block_of(above))
    permute([(block_of(below), HALF, HALF), (block_of(above), 0, HALF)])
    relay_a.wait_recv()
    relay_b.wait_recv()
    permute([(block_of(below, 1 - core), HALF, HALF), (block_of(above, 1 - core), 0, HALF)])

    relay_a, relay_b = stage(forward_up, 0, forward_down, 1, block_of(across), block_of(across))
    mix_across = [send(mix_z, mix_y.at[o], at(y_=y_off(o))) for o in (1, 2, 3)]
    permute([(block_of(across), 0, ROWS)])
    relay_a.wait_recv()
    relay_b.wait_recv()
    permute([(block_of(across, 1 - core), 0, ROWS)])

    got_inverse.wait()
    solved = jnp.dot(inverse[...], ordered[...], preferred_element_type=jnp.float32)
    live = first_row + lax.broadcasted_iota(jnp.int32, (ROWS, CASES), 0) < size
    field[...] = jnp.where(live, solved, 0.0).T

    def split_dot(value, weight):
        high = value.astype(jnp.bfloat16)
        low = (value - high.astype(jnp.float32)).astype(jnp.bfloat16)
        return jnp.dot(high, weight, preferred_element_type=jnp.float32) + jnp.dot(
            low, weight, preferred_element_type=jnp.float32
        )

    coef[...] = split_dot(field[...], right_w[...])
    to_core = send(coef.at[pl.ds(pl.multiple_of(128 * (1 - core), 128), 128), :], in_core, sibling)

    for copy in mix_across:
        copy.wait_recv()
    mine = pl.ds(pl.multiple_of(64 * core + 16 * z_lo, 16), 16)
    mixing[mine, :] = mix_z[...] + mix_y[1] + mix_y[2] + mix_y[3]
    spread = [send(mixing.at[mine, :], mixing.at[mine, :], at(z_=other)) for other in near_z]
    spread += [
        send(mixing.at[mine, :], mixing.at[mine, :], at(z_=other, core_=1 - core))
        for other in [z] + near_z
    ]

    to_core.wait_recv()
    coef_core[...] = coef[pl.ds(pl.multiple_of(128 * core, 128), 128), :] + in_core[...]
    to_y = [
        send(coef_core.at[pl.ds(pl.multiple_of(32 * y_off(o), 32), 32), :], in_y.at[o], at(y_=y_off(o)))
        for o in (1, 2, 3)
    ]
    for copy in to_y:
        copy.wait_recv()
    coef_y[...] = coef_core[pl.ds(pl.multiple_of(32 * y, 32), 32), :] + in_y[1] + in_y[2] + in_y[3]
    to_z = [
        send(
            coef_y.at[pl.ds(pl.multiple_of(8 * lax.rem(z_lo + o, 4), 8), 8), :], in_z.at[o],
            at(z_=z_off(o)),
        )
        for o in (1, 2, 3)
    ]
    for copy in spread:
        copy.wait_recv()
    for copy in to_z:
        copy.wait_recv()
    coef_mine[...] = coef_y[pl.ds(pl.multiple_of(8 * z_lo, 8), 8), :] + in_z[1] + in_z[2] + in_z[3]

    def exact_dot(value, weight):
        return jnp.dot(value, weight, precision=lax.Precision.HIGHEST, preferred_element_type=jnp.float32)

    zero = coef_mine[:, :RANK]
    sent[0] = zero
    to_node = [send(sent.at[0], in_node.at[0], at(z_=z_off(0, 1)))]
    mixed = exact_dot(zero, mixing[:, :2 * RANK])
    one = coef_mine[:, RANK:2 * RANK] + mixed[:, :RANK]
    sent[1] = one
    to_node += [send(sent.at[1], in_node.at[1 + f], at(x_=x_pair, z_=z_off(0, f))) for f in range(2)]
    sent[2] = coef_mine[:, 2 * RANK:] + mixed[:, RANK:] + exact_dot(one, mixing[:, 2 * RANK:])
    to_node += [
        send(sent.at[2], in_node.at[3 + 2 * g + f], at(x_=far, z_=z_off(0, f)))
        for g, far in enumerate(x_far) for f in range(2)
    ]
    for copy in to_node:
        copy.wait_recv()
    eight = pl.ds(pl.multiple_of(128 * core + 32 * y + 8 * z_lo, 8), 8)
    partner[eight, :RANK] = in_node[0]
    partner[eight, RANK:2 * RANK] = in_node[1] + in_node[2]
    partner[eight, 2 * RANK:] = (in_node[3] + in_node[4]) + (in_node[5] + in_node[6])
    back = [send(partner.at[eight, :], partner.at[eight, :], at(z_=other)) for other in near_z]
    for copy in back:
        copy.wait_recv()
    many = pl.ds(pl.multiple_of(128 * core + 32 * y, 32), 32)
    back = [send(partner.at[many, :], partner.at[many, :], at(y_=y_off(o))) for o in (1, 2, 3)]
    for copy in back:
        copy.wait_recv()
    most = pl.ds(pl.multiple_of(128 * core, 128), 128)
    back = send(partner.at[most, :], partner.at[most, :], sibling)
    back.wait_recv()
    out_ref[...] = field[...] + split_dot(partner[...], left_t[...])
    for copy in copies:
        copy.wait_send()


def body(loads, leaf_sizes, tree_order, leaf_inverse, left_factors, right_factors):
    f32, bf16 = jnp.float32, jnp.bfloat16
    scratch = [
        ((CASES, ROWS), bf16),
        ((8, ROWS, CASES), bf16),
        ((32, 128), jnp.int32),
        ((SLOTS, 128), jnp.int32),
        ((SLOTS, CASES), bf16),
        ((ROWS, SLOTS), bf16),
        ((LEVELS, ROWS, RANK), bf16),
        ((LEVELS, ROWS, RANK), bf16),
        ((WIDE, ROWS), bf16),
        ((ROWS, WIDE), bf16),
        ((CASES, ROWS), f32),
        ((CASES, WIDE), f32),
        ((128, WIDE), f32),
        ((32, WIDE), f32),
        ((8, WIDE), f32),
        ((128, WIDE), f32),
        ((4, 32, WIDE), f32),
        ((4, 8, WIDE), f32),
        ((3, 8, RANK), f32),
        ((7, 8, RANK), f32),
        ((CASES, WIDE), f32),
        ((RANK, WIDE), f32),
        ((64, WIDE), f32),
        ((64, WIDE), f32),
        ((4, 16, 2 * RANK), f32),
        ((8, 16, RANK), f32),
        ((16, WIDE), f32),
        ((4, 16, WIDE), f32),
        ((RANK, WIDE), f32),
    ]
    anywhere = pl.BlockSpec(memory_space=pl.ANY)
    return pl.pallas_call(
        kernel,
        out_shape=jax.ShapeDtypeStruct((CASES, ROWS), f32),
        in_specs=[
            anywhere, pl.BlockSpec(memory_space=pltpu.SMEM), anywhere, anywhere, anywhere, anywhere,
        ],
        out_specs=pl.BlockSpec(memory_space=pltpu.VMEM),
        scratch_shapes=[pltpu.VMEM(shape, dtype) for shape, dtype in scratch] + [
            pltpu.SemaphoreType.DMA((5,)),
            pltpu.SemaphoreType.DMA((COPIES,)),
            pltpu.SemaphoreType.DMA((COPIES,)),
        ],
        compiler_params=pltpu.CompilerParams(
            collective_id=0, has_side_effects=True, vmem_limit_bytes=48 << 20
        ),
    )(loads, leaf_sizes, tree_order.reshape(32, 128), leaf_inverse, left_factors, right_factors)


def solution(mesh):
    placed = (
        P(None, ("leaf", "fac")),
        P("leaf"),
        P("leaf", None),
        P(("leaf", "fac"), None),
        P(None, ("leaf", "fac"), None),
        P(None, ("leaf", "fac"), None),
    )
    return jax.shard_map(
        body, mesh=mesh, in_specs=placed, out_specs=P(None, ("leaf", "fac")), check_vma=False
    )
```

time: 358 us -> 67 us (0.19)
  the two profiles are of different devices: /device:TPU:28 before, /device:TPU:1 now
where the time goes in v1:
time: 67 us; the launch traced here: 66.7 us
  Pallas kernels  59.4 us (89%)
  local copies, waits for them, and re-layouts  6.63 us (10%)
  between operations  0.67 us (1%)
    pallas_call x1, Pallas kernels, body(): pl.pallas_call(kernel, out_shape=jax.ShapeDtypeStruct((CASES, ROWS), f32)...  59.4 us
    unnamed x11, local copies, waits for them, and re-layouts  6.63 us

profile of v1, /device:TPU:1, one launch (start us, length us, event | category | flops | bytes accessed | tf_op | source)
XLA Modules:
  0.0 66.7 jit_solution(13366004822145077716)
XLA Ops:
  0.7 0.0 copy-start
  0.7 2.2 %copy-done = bf16[512,4096]{1,0:T(8,128)(2,1)S(1)} copy-done((bf16[512,4096]{1,0:T(8,128)(2,1)S(1)}, bf16[512,4096]{1,0:T(8,128)(2,1)}, u32[]{:S(2)}) %copy-start) | copy-done | bytes 4194328
  2.8 0.0 copy-start.1
  2.8 1.0 %copy-done.1 = bf16[3,512,128]{2,1,0:T(8,128)(2,1)S(1)} copy-done((bf16[3,512,128]{2,1,0:T(8,128)(2,1)S(1)}, bf16[3,512,128]{2,1,0:T(8,128)(2,1)}, u32[]{:S(2)}) %copy-start.1) | copy-done | bytes 393240
  3.8 0.0 copy-start.2
  3.8 1.0 %copy-done.2 = bf16[3,512,128]{2,1,0:T(8,128)(2,1)S(1)} copy-done((bf16[3,512,128]{2,1,0:T(8,128)(2,1)S(1)}, bf16[3,512,128]{2,1,0:T(8,128)(2,1)}, u32[]{:S(2)}) %copy-start.2) | copy-done | bytes 393240
  4.8 0.0 copy-start.3
  4.8 0.9 %copy-done.3 = bf16[256,512]{1,0:T(8,128)(2,1)S(1)} copy-done((bf16[256,512]{1,0:T(8,128)(2,1)S(1)}, bf16[256,512]{1,0:T(8,128)(2,1)}, u32[]{:S(2)}) %copy-start.3) | copy-done | bytes 262168
  5.8 0.0 copy-start.4
  5.8 0.7 %copy-done.4 = s32[1,4096]{1,0:T(1,128)S(1)} copy-done((s32[1,4096]{1,0:T(1,128)S(1)}, s32[1,4096]{1,0:T(1,128)}, u32[]{:S(2)}) %copy-start.4) | copy-done | bytes 16408
  6.5 59.4 %shard_map.64 = f32[256,512]{1,0:T(8,128)S(1)} custom-call(bf16[256,512]{1,0:T(8,128)(2,1)S(1)} %copy-done.3, s32[1]{0:T(128)S(6)} %copy.8.size_ref, s32[32,128]{1,0:T(8,128)S(1)} %bitcast.1, bf16[512,4096]{1,0:T(8,128)(2,1)S(1)} %copy-done, bf16[3,512,128]{2,1,0:T(8,128)(2,1)S(1)} %copy-done.1, bf16[3,512,128]{2,1,0:T(8,128)(2,1)S(1)} %copy-done.2), custom_call_target="tpu_custom_call" | custom-call | tf_op jit(solution)/shard_map/pallas_call | solution.py:322
  65.9 0.8 %copy.9 = f32[256,512]{1,0:T(8,128)} copy(f32[256,512]{1,0:T(8,128)S(1)} %shard_map.64) | data formatting | bytes 1048576
Async XLA Ops:
  0.7 2.2 %copy-start = (bf16[512,4096]{1,0:T(8,128)(2,1)S(1)}, bf16[512,4096]{1,0:T(8,128)(2,1)}, u32[]{:S(2)}) copy-start(bf16[512,4096]{1,0:T(8,128)(2,1)} %inverse_ref.1) | copy-start | bytes 12582916
  2.8 1.0 %copy-start.1 = (bf16[3,512,128]{2,1,0:T(8,128)(2,1)S(1)}, bf16[3,512,128]{2,1,0:T(8,128)(2,1)}, u32[]{:S(2)}) copy-start(bf16[3,512,128]{2,1,0:T(8,128)(2,1)} %left_ref.1) | copy-start | bytes 1179652
  3.8 1.0 %copy-start.2 = (bf16[3,512,128]{2,1,0:T(8,128)(2,1)S(1)}, bf16[3,512,128]{2,1,0:T(8,128)(2,1)}, u32[]{:S(2)}) copy-start(bf16[3,512,128]{2,1,0:T(8,128)(2,1)} %right_ref.1) | copy-start | bytes 1179652
  4.8 0.9 %copy-start.3 = (bf16[256,512]{1,0:T(8,128)(2,1)S(1)}, bf16[256,512]{1,0:T(8,128)(2,1)}, u32[]{:S(2)}) copy-start(bf16[256,512]{1,0:T(8,128)(2,1)} %loads_ref.1) | copy-start | bytes 786436
  5.8 0.7 %copy-start.4 = (s32[1,4096]{1,0:T(1,128)S(1)}, s32[1,4096]{1,0:T(1,128)}, u32[]{:S(2)}) copy-start(s32[1,4096]{1,0:T(1,128)} %param.8) | copy-start | bytes 49156

commit v2 on v1

v2 whole, which is shorter than its diff:
```python
import functools

import jax
import jax.numpy as jnp
from jax import lax
from jax.experimental import pallas as pl
from jax.experimental.pallas import tpu as pltpu
from jax.sharding import PartitionSpec as P

CASES = 256
RANK = 128
LEVELS = 3
SLOTS = 4096
ROWS = 512
HALF = 256
WIDE = LEVELS * RANK
COPIES = 64
MESH = pl.DeviceIdType.MESH


def kernel(
    loads_ref, size_ref, order_ref, inverse_ref, left_ref, right_ref, out_ref,
    blocks, order, match, ordered, inverse, other_inverse, left, right, left_t, right_w,
    partial, from_core, field, coef, in_core, coef_core, in_y, coef_y, in_z, coef_mine,
    sent, in_node, partner,
    mix, mix_core, mix_half, mix_near, mix_far, mix_z, mix_y, mixing, mix_split,
    local_sem, send_sem, recv_sem,
):
    leaf, fac = lax.axis_index("leaf"), lax.axis_index("fac")
    x, z = lax.div(leaf, 8), lax.rem(leaf, 8)
    y, core = lax.div(fac, 2), lax.rem(fac, 2)
    z_hi, z_lo = lax.div(z, 4), lax.rem(z, 4)
    x_pair = x + 1 - 2 * lax.rem(x, 2)
    x_far = [lax.rem(x + 2, 4), 3 - x]

    def at(x_=x, z_=z, y_=y, core_=core):
        return (x_ * 8 + z_, y_ * 2 + core_)

    def y_off(o):
        return lax.rem(y + o, 4)

    def z_off(o, flip=0):
        return lax.rem(z_hi + flip, 2) * 4 + lax.rem(z_lo + o, 4)

    def rows_of(start, count):
        return pl.ds(pl.multiple_of(start, 8), count)

    sibling = at(core_=1 - core)
    near_z = [z_off(o) for o in (1, 2, 3)]
    flip_z = [z_off(o, 1) for o in range(4)]
    z_all = [z_off(o, f) for f in range(2) for o in range(4)]
    partners = [at(y_=y_off(o)) for o in (1, 3, 2)]
    partners += [sibling]
    partners += [at(z_=other) for other in near_z + flip_z]
    partners += [at(x_=x_pair, z_=other) for other in z_all]
    partners += [at(x_=far, z_=z_off(0, f)) for far in x_far for f in range(2)]

    barrier = pltpu.get_barrier_semaphore()
    for other in partners:
        pl.semaphore_signal(barrier, inc=1, device_id=other, device_id_type=MESH)

    copies = []

    def send(src, dst, target):
        i = len(copies)
        copy = pltpu.make_async_remote_copy(
            src_ref=src, dst_ref=dst, send_sem=send_sem.at[i], recv_sem=recv_sem.at[i],
            device_id=target, device_id_type=MESH,
        )
        copies.append(copy)
        copy.start()
        return copy

    def recv(copy):
        copy.wait_recv()

    def fetch(i, src, dst):
        copy = pltpu.make_async_copy(src, dst, local_sem.at[i])
        copy.start()
        return copy

    got_order = fetch(1, order_ref, order)
    got_loads = fetch(0, loads_ref, blocks.at[3])
    got_left = fetch(2, left_ref, left)
    got_right = fetch(3, right_ref, right)

    pl.semaphore_wait(barrier, len(partners))

    def columns(ref, start, count):
        return ref.at[:, pl.ds(start, count)]

    up, down = at(y_=y_off(1)), at(y_=y_off(3))
    up_first = send(columns(loads_ref, 0, HALF), columns(blocks.at[0], 0, HALF), up)
    down_first = send(columns(loads_ref, HALF, HALF), columns(blocks.at[1], HALF, HALF), down)
    up_second = send(columns(loads_ref, HALF, HALF), columns(blocks.at[0], HALF, HALF), up)
    down_second = send(columns(loads_ref, 0, HALF), columns(blocks.at[1], 0, HALF), down)
    size = size_ref[0]
    first_row = fac * ROWS
    got_left.wait()
    got_right.wait()
    for level in range(LEVELS):
        live = first_row + lax.broadcasted_iota(jnp.int32, (RANK, ROWS), 1) < size
        turned = left[level].T
        left_t[level * RANK:(level + 1) * RANK, :] = jnp.where(live, turned, jnp.zeros_like(turned))
        right_w[:, level * RANK:(level + 1) * RANK] = right[level]
    mix[:, :2 * RANK] = jnp.dot(left_t[:RANK, :], right_w[:, RANK:], preferred_element_type=jnp.float32)
    mix[:, 2 * RANK:] = jnp.dot(left_t[RANK:2 * RANK, :], right_w[:, 2 * RANK:], preferred_element_type=jnp.float32)
    mix_sib = send(mix.at[rows_of(64 * (1 - core), 64), :], mix_core, sibling)

    inverse_sib = []
    for j in range(2):
        rows = pl.ds(j * HALF, HALF)
        inverse_sib.append(send(inverse_ref.at[rows, :], other_inverse.at[rows, :], sibling))
    got_inverse = fetch(4, inverse_ref, inverse)

    got_order.wait()

    @pl.loop(0, 32)
    def _(r):
        place = r * 128 + lax.broadcasted_iota(jnp.int32, (1, 128), 1)
        row = jnp.where(place < size, order[pl.ds(r, 1), :], -1)
        match[pl.ds(pl.multiple_of(r * 128, 128), 128), :] = jnp.broadcast_to(row, (128, 128)).T

    owners = [y_off(3) * 2 + core, y_off(1) * 2 + core, y_off(2) * 2 + core, fac]

    def permute(parts, first=False):
        @pl.loop(0, 2)
        def _(m):
            rows = pl.ds(pl.multiple_of(m * 2048, 2048), 2048)
            slot = match[rows, :]
            total = None
            for block, start, count in parts:
                picks = []
                for j in range(count // 128):
                    here = owners[block] * ROWS + start + j * 128
                    column = here + lax.broadcasted_iota(jnp.int32, (2048, 128), 1)
                    picks.append(jnp.where(slot == column, 1.0, 0.0).astype(jnp.bfloat16))
                picks = picks[0] if len(picks) == 1 else jnp.concatenate(picks, axis=1)
                term = lax.dot_general(
                    picks, blocks[block, :, start:start + count], (((1,), (1,)), ((), ())),
                    preferred_element_type=jnp.float32,
                )
                total = term if total is None else total + term
            total = total.astype(jnp.bfloat16)
            if first:
                ordered[rows, :] = total
            else:
                ordered[rows, :] += total

    recv(mix_sib)
    mix_half[...] = mix[rows_of(64 * core, 64), :] + mix_core[...]
    to_z = []
    for o in range(4):
        rows = rows_of(16 * lax.rem(z_lo + o, 4), 16)
        to_z.append(send(mix_half.at[rows, pl.ds(0, 2 * RANK)], mix_near.at[o], at(z_=z_off(o, 1))))
        for f in range(2):
            to_z.append(send(
                mix_half.at[rows, pl.ds(2 * RANK, RANK)], mix_far.at[f * 4 + o],
                at(x_=x_pair, z_=z_off(o, f)),
            ))

    got_loads.wait()
    permute([(3, 0, ROWS)], first=True)

    forwards = []
    quarter = HALF // 2
    recv(up_first)
    for j in range(2):
        here = j * quarter
        forwards.append(send(columns(blocks.at[0], here, quarter), columns(blocks.at[2], here, quarter), up))
    recv(down_first)
    for j in range(2):
        here = HALF + (1 - j) * quarter
        forwards.append(send(columns(blocks.at[1], here, quarter), columns(blocks.at[2], here, quarter), down))
    permute([(0, 0, HALF), (1, HALF, HALF)])

    recv(up_second)
    recv(down_second)
    permute([(0, HALF, HALF), (1, 0, HALF)])

    for copy in to_z:
        recv(copy)
    mix_z[:, :2 * RANK] = mix_near[0] + mix_near[1] + mix_near[2] + mix_near[3]
    far = mix_far[0]
    for j in range(1, 8):
        far = far + mix_far[j]
    mix_z[:, 2 * RANK:] = far
    mix_across = [send(mix_z, mix_y.at[o], at(y_=y_off(o))) for o in (1, 2, 3)]

    recv(forwards[0])
    recv(forwards[2])
    permute([(2, 0, quarter), (2, 3 * quarter, quarter)])
    recv(forwards[1])
    recv(forwards[3])
    permute([(2, quarter, HALF)])

    to_core = []
    for j in range(2):
        rows = pl.ds(j * HALF, HALF)
        recv(inverse_sib[j])
        partial[rows, :] = jnp.dot(other_inverse[rows, :], ordered[...], preferred_element_type=jnp.float32)
        to_core.append(send(partial.at[rows, :], from_core.at[rows, :], sibling))

    got_inverse.wait()
    solved = jnp.dot(inverse[...], ordered[...], preferred_element_type=jnp.float32)
    for copy in to_core:
        recv(copy)
    live = first_row + lax.broadcasted_iota(jnp.int32, (ROWS, CASES), 0) < size
    field[...] = jnp.where(live, solved + from_core[...], 0.0).T

    def halves(value):
        high = value.astype(jnp.bfloat16)
        return high, (value - high.astype(jnp.float32)).astype(jnp.bfloat16)

    def split_dot(value, weight):
        high, low = halves(value)
        return jnp.dot(high, weight, preferred_element_type=jnp.float32) + jnp.dot(
            low, weight, preferred_element_type=jnp.float32
        )

    theirs, ours = rows_of(128 * (1 - core), 128), rows_of(128 * core, 128)
    coef[...] = split_dot(field[theirs, :], right_w[...])
    coef_sib = send(coef, in_core, sibling)
    own_coef = split_dot(field[ours, :], right_w[...])
    for copy in mix_across:
        recv(copy)
    mine = rows_of(64 * core + 16 * z_lo, 16)
    mixing[mine, :] = mix_z[...] + mix_y[1] + mix_y[2] + mix_y[3]
    spread = [send(mixing.at[mine, :], mixing.at[mine, :], at(z_=other)) for other in near_z]
    recv(coef_sib)
    coef_core[...] = own_coef + in_core[...]
    to_y = [
        send(coef_core.at[rows_of(32 * y_off(o), 32), :], in_y.at[o], at(y_=y_off(o)))
        for o in (2, 1, 3)
    ]
    for copy in spread:
        recv(copy)
    sixty_four = mixing.at[rows_of(64 * core, 64), :]
    spread = send(sixty_four, sixty_four, sibling)
    for copy in to_y:
        recv(copy)
    coef_y[...] = coef_core[rows_of(32 * y, 32), :] + in_y[1] + in_y[2] + in_y[3]
    to_z = [
        send(coef_y.at[rows_of(8 * lax.rem(z_lo + o, 4), 8), :], in_z.at[o], at(z_=z_off(o)))
        for o in (1, 2, 3)
    ]
    recv(spread)
    mix_split[:, :WIDE], mix_split[:, WIDE:] = halves(mixing[...])
    for copy in to_z:
        recv(copy)
    coef_mine[...] = coef_y[rows_of(8 * z_lo, 8), :] + in_z[1] + in_z[2] + in_z[3]

    def mixed(value, start, count):
        high, low = halves(value)
        both = jnp.concatenate([high, low], axis=0)
        by_high = jnp.dot(both, mix_split[:, start:start + count], preferred_element_type=jnp.float32)
        by_low = jnp.dot(both, mix_split[:, WIDE + start:WIDE + start + count], preferred_element_type=jnp.float32)
        return by_high[:8] + (by_high[8:] + by_low[:8])

    zero = coef_mine[:, :RANK]
    sent[0] = zero
    to_node = [send(sent.at[0], in_node.at[0], at(z_=z_off(0, 1)))]
    terms = mixed(zero, 0, 2 * RANK)
    one = coef_mine[:, RANK:2 * RANK] + terms[:, :RANK]
    sent[1] = one
    to_node += [send(sent.at[1], in_node.at[1 + f], at(x_=x_pair, z_=z_off(0, f))) for f in range(2)]
    sent[2] = coef_mine[:, 2 * RANK:] + terms[:, RANK:] + mixed(one, 2 * RANK, RANK)
    to_node += [
        send(sent.at[2], in_node.at[3 + 2 * g + f], at(x_=far, z_=z_off(0, f)))
        for g, far in enumerate(x_far) for f in range(2)
    ]
    for copy in to_node:
        recv(copy)
    eight = rows_of(128 * core + 32 * y + 8 * z_lo, 8)
    partner[eight, :RANK] = in_node[0]
    partner[eight, RANK:2 * RANK] = in_node[1] + in_node[2]
    partner[eight, 2 * RANK:] = (in_node[3] + in_node[4]) + (in_node[5] + in_node[6])
    back = [send(partner.at[eight, :], partner.at[eight, :], at(z_=other)) for other in near_z]
    for copy in back:
        recv(copy)

    def thirty_two(y_):
        return partner.at[rows_of(128 * core + 32 * y_, 32), :]

    back = [(send(thirty_two(y), thirty_two(y), at(y_=y_off(o))), y_off(4 - o)) for o in (2, 1, 3)]
    relays = [send(thirty_two(y), thirty_two(y), sibling)]
    for copy, y_ in back[1:] + back[:1]:
        recv(copy)
        relays.append(send(thirty_two(y_), thirty_two(y_), sibling))
    out_ref[ours, :] = field[ours, :] + split_dot(partner[ours, :], left_t[...])
    for copy in relays:
        recv(copy)
    out_ref[theirs, :] = field[theirs, :] + split_dot(partner[theirs, :], left_t[...])
    for copy in copies:
        copy.wait_send()


def body(loads, leaf_sizes, tree_order, leaf_inverse, left_factors, right_factors):
    f32, bf16 = jnp.float32, jnp.bfloat16
    scratch = [
        ((4, CASES, ROWS), bf16),
        ((32, 128), jnp.int32),
        ((SLOTS, 128), jnp.int32),
        ((SLOTS, CASES), bf16),
        ((ROWS, SLOTS), bf16),
        ((ROWS, SLOTS), bf16),
        ((LEVELS, ROWS, RANK), bf16),
        ((LEVELS, ROWS, RANK), bf16),
        ((WIDE, ROWS), bf16),
        ((ROWS, WIDE), bf16),
        ((ROWS, CASES), f32),
        ((ROWS, CASES), f32),
        ((CASES, ROWS), f32),
        ((128, WIDE), f32),
        ((128, WIDE), f32),
        ((128, WIDE), f32),
        ((4, 32, WIDE), f32),
        ((32, WIDE), f32),
        ((4, 8, WIDE), f32),
        ((8, WIDE), f32),
        ((3, 8, RANK), f32),
        ((7, 8, RANK), f32),
        ((CASES, WIDE), f32),
        ((RANK, WIDE), f32),
        ((64, WIDE), f32),
        ((64, WIDE), f32),
        ((4, 16, 2 * RANK), f32),
        ((8, 16, RANK), f32),
        ((16, WIDE), f32),
        ((4, 16, WIDE), f32),
        ((RANK, WIDE), f32),
        ((RANK, 2 * WIDE), bf16),
    ]
    in_hbm = pl.BlockSpec(memory_space=pltpu.HBM)
    return pl.pallas_call(
        kernel,
        out_shape=pltpu.VMEM((CASES, ROWS), f32),
        in_specs=[
            in_hbm, pl.BlockSpec(memory_space=pltpu.SMEM), in_hbm, in_hbm, in_hbm, in_hbm,
        ],
        out_specs=pl.BlockSpec(memory_space=pltpu.VMEM),
        scratch_shapes=[pltpu.VMEM(shape, dtype) for shape, dtype in scratch] + [
            pltpu.SemaphoreType.DMA((5,)),
            pltpu.SemaphoreType.DMA((COPIES,)),
            pltpu.SemaphoreType.DMA((COPIES,)),
        ],
        compiler_params=pltpu.CompilerParams(
            collective_id=0, has_side_effects=True, vmem_limit_bytes=60 << 20
        ),
    )(loads, leaf_sizes, tree_order.reshape(32, 128), leaf_inverse, left_factors, right_factors)


def solution(mesh):
    placed = (
        P(None, ("leaf", "fac")),
        P("leaf"),
        P("leaf", None),
        P(("leaf", "fac"), None),
        P(None, ("leaf", "fac"), None),
        P(None, ("leaf", "fac"), None),
    )
    return jax.shard_map(
        body, mesh=mesh, in_specs=placed, out_specs=P(None, ("leaf", "fac")), check_vma=False
    )
```

time: 67 us -> 57.8 us (0.86)
  local copies, waits for them, and re-layouts: 6.63 us -> 0.8 us
  Pallas kernels: 59.4 us -> 56.3 us
    unnamed x11 -> x1, local copies, waits for them, and re-layouts: 6.63 us -> 0.8 us
    pallas_call x1, Pallas kernels: 59.4 us -> 56.3 us  [body(): pl.pallas_call(kernel, out_shape=pltpu.VMEM((CASES, ROWS), f32), in_specs...]
where the time goes in v2:
time: 57.8 us
  Pallas kernels  56.3 us (97%)
  local copies, waits for them, and re-layouts  0.8 us (1%)
  between operations  0.66 us (1%)
    pallas_call x1, Pallas kernels, body(): pl.pallas_call(kernel, out_shape=pltpu.VMEM((CASES, ROWS), f32), in_specs...  56.3 us

profile of v2, /device:TPU:1, one launch (start us, length us, event | category | flops | bytes accessed | tf_op | source)
XLA Modules:
  0.0 57.8 jit_solution(10640797642287761089)
XLA Ops:
  0.7 56.3 %shard_map.64 = f32[256,512]{1,0:T(8,128)S(1)} custom-call(bf16[256,512]{1,0:T(8,128)(2,1)} %loads_ref.1, s32[1]{0:T(128)S(6)} %copy.9.size_ref, s32[32,128]{1,0:T(8,128)} %bitcast.1, bf16[512,4096]{1,0:T(8,128)(2,1)} %inverse_ref.1, bf16[3,512,128]{2,1,0:T(8,128)(2,1)} %left_ref.1, bf16[3,512,128]{2,1,0:T(8,128)(2,1)} %right_ref.1), custom_call_target="tpu_custom_call" | custom-call | tf_op jit(solution)/shard_map/pallas_call | solution.py:335
  57.0 0.8 %copy.8 = f32[256,512]{1,0:T(8,128)} copy(f32[256,512]{1,0:T(8,128)S(1)} %shard_map.64) | data formatting | bytes 1048576

commit v3 on v2

--- a/solution.py
+++ b/solution.py
@@ -14,15 +14,14 @@
 ROWS = 512
 HALF = 256
 WIDE = LEVELS * RANK
-COPIES = 64
+COPIES = 96
 MESH = pl.DeviceIdType.MESH
 
 
 def kernel(
     loads_ref, size_ref, order_ref, inverse_ref, left_ref, right_ref, out_ref,
     blocks, order, match, ordered, inverse, other_inverse, left, right, left_t, right_w,
-    partial, from_core, field, coef, in_core, coef_core, in_y, coef_y, in_z, coef_mine,
-    sent, in_node, partner,
+    partial, from_core, field, coef, in_core, coef_core, in_y, coef_y, node, in_flip, in_near, in_zero, in_one, in_two, partner,
     mix, mix_core, mix_half, mix_near, mix_far, mix_z, mix_y, mixing, mix_split,
     local_sem, send_sem, recv_sem,
 ):
@@ -51,9 +50,10 @@
     z_all = [z_off(o, f) for f in range(2) for o in range(4)]
     partners = [at(y_=y_off(o)) for o in (1, 3, 2)]
     partners += [sibling]
+    partners += [at(y_=y_off(o), core_=1 - core) for o in (1, 2, 3)]
     partners += [at(z_=other) for other in near_z + flip_z]
     partners += [at(x_=x_pair, z_=other) for other in z_all]
-    partners += [at(x_=far, z_=z_off(0, f)) for far in x_far for f in range(2)]
+    partners += [at(x_=far, z_=other) for far in x_far for other in [z] + near_z]
 
     barrier = pltpu.get_barrier_semaphore()
     for other in partners:
@@ -115,11 +115,10 @@
 
     got_order.wait()
 
-    @pl.loop(0, 32)
-    def _(r):
-        place = r * 128 + lax.broadcasted_iota(jnp.int32, (1, 128), 1)
-        row = jnp.where(place < size, order[pl.ds(r, 1), :], -1)
-        match[pl.ds(pl.multiple_of(r * 128, 128), 128), :] = jnp.broadcast_to(row, (128, 128)).T
+    place = lax.broadcasted_iota(jnp.int32, (32, 128), 0) * 128 + lax.broadcasted_iota(jnp.int32, (32, 128), 1)
+    turned = jnp.where(place < size, order[...], -1).T
+    for r in range(32):
+        match[r * 128:(r + 1) * 128, :] = jnp.broadcast_to(turned[:, r:r + 1], (128, 128))
 
     owners = [y_off(3) * 2 + core, y_off(1) * 2 + core, y_off(2) * 2 + core, fac]
 
@@ -201,6 +200,11 @@
         partial[rows, :] = jnp.dot(other_inverse[rows, :], ordered[...], preferred_element_type=jnp.float32)
         to_core.append(send(partial.at[rows, :], from_core.at[rows, :], sibling))
 
+    for copy in mix_across:
+        recv(copy)
+    mine = rows_of(64 * core + 16 * z_lo, 16)
+    mixing[mine, :] = mix_z[...] + mix_y[1] + mix_y[2] + mix_y[3]
+    spread = [send(mixing.at[mine, :], mixing.at[mine, :], at(z_=other)) for other in near_z]
     got_inverse.wait()
     solved = jnp.dot(inverse[...], ordered[...], preferred_element_type=jnp.float32)
     for copy in to_core:
@@ -222,71 +226,76 @@
     coef[...] = split_dot(field[theirs, :], right_w[...])
     coef_sib = send(coef, in_core, sibling)
     own_coef = split_dot(field[ours, :], right_w[...])
-    for copy in mix_across:
-        recv(copy)
-    mine = rows_of(64 * core + 16 * z_lo, 16)
-    mixing[mine, :] = mix_z[...] + mix_y[1] + mix_y[2] + mix_y[3]
-    spread = [send(mixing.at[mine, :], mixing.at[mine, :], at(z_=other)) for other in near_z]
     recv(coef_sib)
     coef_core[...] = own_coef + in_core[...]
-    to_y = [
-        send(coef_core.at[rows_of(32 * y_off(o), 32), :], in_y.at[o], at(y_=y_off(o)))
-        for o in (2, 1, 3)
-    ]
+    pair = lax.div(z_lo, 2)
+    to_y = []
+    for part in (1 - pair, pair):
+        for o in (2, 1, 3):
+            rows = rows_of(32 * y_off(o) + 16 * part, 16)
+            to_y.append(send(coef_core.at[rows, :], in_y.at[o, rows_of(16 * part, 16), :], at(y_=y_off(o))))
     for copy in spread:
         recv(copy)
     sixty_four = mixing.at[rows_of(64 * core, 64), :]
     spread = send(sixty_four, sixty_four, sibling)
-    for copy in to_y:
-        recv(copy)
-    coef_y[...] = coef_core[rows_of(32 * y, 32), :] + in_y[1] + in_y[2] + in_y[3]
-    to_z = [
-        send(coef_y.at[rows_of(8 * lax.rem(z_lo + o, 4), 8), :], in_z.at[o], at(z_=z_off(o)))
-        for o in (1, 2, 3)
-    ]
-    recv(spread)
-    mix_split[:, :WIDE], mix_split[:, WIDE:] = halves(mixing[...])
-    for copy in to_z:
-        recv(copy)
-    coef_mine[...] = coef_y[rows_of(8 * z_lo, 8), :] + in_z[1] + in_z[2] + in_z[3]
+
+    def z_flip(o):
+        return [z_lo, z_lo + 1 - 2 * lax.rem(z_lo, 2), lax.rem(z_lo + 2, 4), 3 - z_lo][o]
 
     def mixed(value, start, count):
         high, low = halves(value)
         both = jnp.concatenate([high, low], axis=0)
         by_high = jnp.dot(both, mix_split[:, start:start + count], preferred_element_type=jnp.float32)
         by_low = jnp.dot(both, mix_split[:, WIDE + start:WIDE + start + count], preferred_element_type=jnp.float32)
-        return by_high[:8] + (by_high[8:] + by_low[:8])
-
-    zero = coef_mine[:, :RANK]
-    sent[0] = zero
-    to_node = [send(sent.at[0], in_node.at[0], at(z_=z_off(0, 1)))]
-    terms = mixed(zero, 0, 2 * RANK)
-    one = coef_mine[:, RANK:2 * RANK] + terms[:, :RANK]
-    sent[1] = one
-    to_node += [send(sent.at[1], in_node.at[1 + f], at(x_=x_pair, z_=z_off(0, f))) for f in range(2)]
-    sent[2] = coef_mine[:, 2 * RANK:] + terms[:, RANK:] + mixed(one, 2 * RANK, RANK)
-    to_node += [
-        send(sent.at[2], in_node.at[3 + 2 * g + f], at(x_=far, z_=z_off(0, f)))
-        for g, far in enumerate(x_far) for f in range(2)
-    ]
+        return by_high[:16] + (by_high[16:] + by_low[:16])
+
+    recv(spread)
+    mix_split[:, :WIDE], mix_split[:, WIDE:] = halves(mixing[...])
+    to_node = []
+    for n, part in enumerate((1 - pair, pair)):
+        for copy in to_y[3 * n:3 * n + 3]:
+            recv(copy)
+        rows = rows_of(16 * part, 16)
+        summed = coef_core[rows_of(32 * y + 16 * part, 16), :] + in_y[1, rows, :] + in_y[2, rows, :] + in_y[3, rows, :]
+        zero = summed[:, :RANK]
+        terms = mixed(zero, 0, 2 * RANK)
+        one = summed[:, RANK:2 * RANK] + terms[:, :RANK]
+        two = summed[:, 2 * RANK:] + terms[:, RANK:] + mixed(one, 2 * RANK, RANK)
+        coef_y[rows, :] = jnp.concatenate([zero, one, two], axis=1)
+        for o in ((2, 3), (0, 1))[n]:
+            eight = rows_of(8 * z_flip(o), 8)
+            there = z_hi * 4 + z_flip(o)
+            for g, far in enumerate(x_far):
+                to_node.append(send(coef_y.at[eight, pl.ds(2 * RANK, RANK)], in_two.at[o, g], at(x_=far, z_=there)))
+            to_node.append(send(coef_y.at[eight, pl.ds(RANK, RANK)], in_one.at[o], at(x_=x_pair, z_=there)))
+            if o:
+                to_node.append(send(coef_y.at[eight, pl.ds(0, RANK)], in_zero.at[o], at(z_=there)))
     for copy in to_node:
         recv(copy)
-    eight = rows_of(128 * core + 32 * y + 8 * z_lo, 8)
-    partner[eight, :RANK] = in_node[0]
-    partner[eight, RANK:2 * RANK] = in_node[1] + in_node[2]
-    partner[eight, 2 * RANK:] = (in_node[3] + in_node[4]) + (in_node[5] + in_node[6])
-    back = [send(partner.at[eight, :], partner.at[eight, :], at(z_=other)) for other in near_z]
-    for copy in back:
-        recv(copy)
+    node[:, :RANK] = coef_y[rows_of(8 * z_lo, 8), :RANK] + (in_zero[1] + in_zero[2] + in_zero[3])
+    node[:, RANK:2 * RANK] = (in_one[0] + in_one[1]) + (in_one[2] + in_one[3])
+    node[:, 2 * RANK:] = ((in_two[0, 0] + in_two[1, 0]) + (in_two[2, 0] + in_two[3, 0])) + (
+        (in_two[0, 1] + in_two[1, 1]) + (in_two[2, 1] + in_two[3, 1])
+    )
+    over = [send(node, in_flip.at[o], at(z_=z_off(o, 1))) for o in range(4)]
+    wide = pl.ds(RANK, 2 * RANK)
+    over += [send(node.at[:, wide], in_near.at[o], at(z_=z_off(o))) for o in (1, 2, 3)]
+    for copy in over:
+        recv(copy)
+    for o in range(4):
+        eight = rows_of(128 * core + 32 * y + 8 * lax.rem(z_lo + 4 - o, 4), 8)
+        beside = node[:, RANK:] if o == 0 else in_near[o]
+        partner[eight, :RANK] = in_flip[o, :, :RANK]
+        partner[eight, RANK:] = in_flip[o, :, RANK:] + beside
 
     def thirty_two(y_):
         return partner.at[rows_of(128 * core + 32 * y_, 32), :]
 
-    back = [(send(thirty_two(y), thirty_two(y), at(y_=y_off(o))), y_off(4 - o)) for o in (2, 1, 3)]
-    relays = [send(thirty_two(y), thirty_two(y), sibling)]
-    for copy, y_ in back[1:] + back[:1]:
-        recv(copy)
-        relays.append(send(thirty_two(y_), thirty_two(y_), sibling))
+    back = [send(thirty_two(y), thirty_two(y), at(y_=y_off(o))) for o in (2, 1, 3)]
+    relays = [send(thirty_two(y), thirty_two(y), at(y_=y_off(o), core_=1 - core)) for o in (2, 1, 3)]
+    relays.append(send(thirty_two(y), thirty_two(y), sibling))
+    for copy in back:
+        recv(copy)
     out_ref[ours, :] = field[ours, :] + split_dot(partner[ours, :], left_t[...])
     for copy in relays:
         recv(copy)
@@ -316,10 +325,12 @@
         ((128, WIDE), f32),
         ((4, 32, WIDE), f32),
         ((32, WIDE), f32),
+        ((8, WIDE), f32),
         ((4, 8, WIDE), f32),
-        ((8, WIDE), f32),
-        ((3, 8, RANK), f32),
-        ((7, 8, RANK), f32),
+        ((4, 8, 2 * RANK), f32),
+        ((4, 8, RANK), f32),
+        ((4, 8, RANK), f32),
+        ((4, 2, 8, RANK), f32),
         ((CASES, WIDE), f32),
         ((RANK, WIDE), f32),
         ((64, WIDE), f32),

time: 57.8 us -> 53.8 us (0.931)
  Pallas kernels: 56.3 us -> 52.2 us
    pallas_call x1, Pallas kernels: 56.3 us -> 52.2 us  [body(): pl.pallas_call(kernel, out_shape=pltpu.VMEM((CASES, ROWS), f32), in_specs...]
where the time goes in v3:
time: 53.8 us; the launch traced here: 53.7 us
  Pallas kernels  52.2 us (97%)
  local copies, waits for them, and re-layouts  0.8 us (1%)
  between operations  0.66 us (1%)
    pallas_call x1, Pallas kernels, body(): pl.pallas_call(kernel, out_shape=pltpu.VMEM((CASES, ROWS), f32), in_specs...  52.2 us

profile of v3, /device:TPU:1, one launch (start us, length us, event | category | flops | bytes accessed | tf_op | source)
XLA Modules:
  0.0 53.7 jit_solution(8124481865370141108)
XLA Ops:
  0.7 52.2 %shard_map.64 = f32[256,512]{1,0:T(8,128)S(1)} custom-call(bf16[256,512]{1,0:T(8,128)(2,1)} %loads_ref.1, s32[1]{0:T(128)S(6)} %copy.9.size_ref, s32[32,128]{1,0:T(8,128)} %bitcast.1, bf16[512,4096]{1,0:T(8,128)(2,1)} %inverse_ref.1, bf16[3,512,128]{2,1,0:T(8,128)(2,1)} %left_ref.1, bf16[3,512,128]{2,1,0:T(8,128)(2,1)} %right_ref.1), custom_call_target="tpu_custom_call" | custom-call | tf_op jit(solution)/shard_map/pallas_call | solution.py:346
  52.9 0.8 %copy.8 = f32[256,512]{1,0:T(8,128)} copy(f32[256,512]{1,0:T(8,128)S(1)} %shard_map.64) | data formatting | bytes 1048576

commit v4 on v3

--- a/solution.py
+++ b/solution.py
@@ -20,8 +20,9 @@
 
 def kernel(
     loads_ref, size_ref, order_ref, inverse_ref, left_ref, right_ref, out_ref,
-    blocks, order, match, ordered, inverse, other_inverse, left, right, left_t, right_w,
-    partial, from_core, field, coef, in_core, coef_core, in_y, coef_y, node, in_flip, in_near, in_zero, in_one, in_two, partner,
+    blocks, order, match, ordered, inverse, left, right, left_t, right_w,
+    partial, from_core, field, coef_core, in_y, coef_y, node, in_flip, in_near,
+    in_zero, in_one, in_two, partner, out_far,
     mix, mix_core, mix_half, mix_near, mix_far, mix_z, mix_y, mixing, mix_split,
     local_sem, send_sem, recv_sem,
 ):
@@ -50,7 +51,6 @@
     z_all = [z_off(o, f) for f in range(2) for o in range(4)]
     partners = [at(y_=y_off(o)) for o in (1, 3, 2)]
     partners += [sibling]
-    partners += [at(y_=y_off(o), core_=1 - core) for o in (1, 2, 3)]
     partners += [at(z_=other) for other in near_z + flip_z]
     partners += [at(x_=x_pair, z_=other) for other in z_all]
     partners += [at(x_=far, z_=other) for far in x_far for other in [z] + near_z]
@@ -101,17 +101,18 @@
     for level in range(LEVELS):
         live = first_row + lax.broadcasted_iota(jnp.int32, (RANK, ROWS), 1) < size
         turned = left[level].T
-        left_t[level * RANK:(level + 1) * RANK, :] = jnp.where(live, turned, jnp.zeros_like(turned))
-        right_w[:, level * RANK:(level + 1) * RANK] = right[level]
-    mix[:, :2 * RANK] = jnp.dot(left_t[:RANK, :], right_w[:, RANK:], preferred_element_type=jnp.float32)
-    mix[:, 2 * RANK:] = jnp.dot(left_t[RANK:2 * RANK, :], right_w[:, 2 * RANK:], preferred_element_type=jnp.float32)
+        left_t[core, level * RANK:(level + 1) * RANK, :] = jnp.where(live, turned, jnp.zeros_like(turned))
+        right_w[core, :, level * RANK:(level + 1) * RANK] = right[level]
+    mix[:, :2 * RANK] = jnp.dot(left_t[core, :RANK, :], right_w[core, :, RANK:], preferred_element_type=jnp.float32)
+    mix[:, 2 * RANK:] = jnp.dot(
+        left_t[core, RANK:2 * RANK, :], right_w[core, :, 2 * RANK:], preferred_element_type=jnp.float32
+    )
     mix_sib = send(mix.at[rows_of(64 * (1 - core), 64), :], mix_core, sibling)
 
-    inverse_sib = []
-    for j in range(2):
-        rows = pl.ds(j * HALF, HALF)
-        inverse_sib.append(send(inverse_ref.at[rows, :], other_inverse.at[rows, :], sibling))
-    got_inverse = fetch(4, inverse_ref, inverse)
+    inverse_sib = send(inverse_ref, inverse.at[core], sibling)
+    right_sib = send(right_w.at[core], right_w.at[core], sibling)
+    left_sib = send(left_t.at[core], left_t.at[core], sibling)
+    got_inverse = fetch(4, inverse_ref, inverse.at[core])
 
     got_order.wait()
 
@@ -122,24 +123,23 @@
 
     owners = [y_off(3) * 2 + core, y_off(1) * 2 + core, y_off(2) * 2 + core, fac]
 
-    def permute(parts, first=False):
-        @pl.loop(0, 2)
+    def permute(parts, first=False, tall=2048):
+        @pl.loop(0, SLOTS // tall)
         def _(m):
-            rows = pl.ds(pl.multiple_of(m * 2048, 2048), 2048)
+            rows = pl.ds(pl.multiple_of(m * tall, tall), tall)
             slot = match[rows, :]
-            total = None
+            picks, held = [], []
             for block, start, count in parts:
-                picks = []
+                held.append(blocks[block, :, start:start + count])
                 for j in range(count // 128):
                     here = owners[block] * ROWS + start + j * 128
-                    column = here + lax.broadcasted_iota(jnp.int32, (2048, 128), 1)
+                    column = here + lax.broadcasted_iota(jnp.int32, (tall, 128), 1)
                     picks.append(jnp.where(slot == column, 1.0, 0.0).astype(jnp.bfloat16))
-                picks = picks[0] if len(picks) == 1 else jnp.concatenate(picks, axis=1)
-                term = lax.dot_general(
-                    picks, blocks[block, :, start:start + count], (((1,), (1,)), ((), ())),
-                    preferred_element_type=jnp.float32,
-                )
-                total = term if total is None else total + term
+            held = held[0] if len(held) == 1 else jnp.concatenate(held, axis=1)
+            total = lax.dot_general(
+                jnp.concatenate(picks, axis=1), held, (((1,), (1,)), ((), ())),
+                preferred_element_type=jnp.float32,
+            )
             total = total.astype(jnp.bfloat16)
             if first:
                 ordered[rows, :] = total
@@ -193,24 +193,28 @@
     recv(forwards[3])
     permute([(2, quarter, HALF)])
 
+    got_inverse.wait()
+    recv(inverse_sib)
     to_core = []
-    for j in range(2):
-        rows = pl.ds(j * HALF, HALF)
-        recv(inverse_sib[j])
-        partial[rows, :] = jnp.dot(other_inverse[rows, :], ordered[...], preferred_element_type=jnp.float32)
-        to_core.append(send(partial.at[rows, :], from_core.at[rows, :], sibling))
-
+
+    def solve(b, start, count):
+        rows = pl.ds(start, count)
+        solved = jnp.dot(inverse[b, rows, :], ordered[...], preferred_element_type=jnp.float32)
+        for h in range(2):
+            partial[h, b, rows, :] = solved[:, 128 * h:128 * h + 128]
+        to_core.append(send(partial.at[1 - core, b, rows, :], from_core.at[b, rows, :], sibling))
+
+    solve(0, 0, ROWS)
+    solve(1, 0, ROWS)
     for copy in mix_across:
         recv(copy)
     mine = rows_of(64 * core + 16 * z_lo, 16)
     mixing[mine, :] = mix_z[...] + mix_y[1] + mix_y[2] + mix_y[3]
     spread = [send(mixing.at[mine, :], mixing.at[mine, :], at(z_=other)) for other in near_z]
-    got_inverse.wait()
-    solved = jnp.dot(inverse[...], ordered[...], preferred_element_type=jnp.float32)
-    for copy in to_core:
-        recv(copy)
-    live = first_row + lax.broadcasted_iota(jnp.int32, (ROWS, CASES), 0) < size
-    field[...] = jnp.where(live, solved + from_core[...], 0.0).T
+
+    def settle(b):
+        live = y * 2 * ROWS + b * ROWS + lax.broadcasted_iota(jnp.int32, (ROWS, 128), 0) < size
+        field[b] = jnp.where(live, partial[core, b] + from_core[b], 0.0).T
 
     def halves(value):
         high = value.astype(jnp.bfloat16)
@@ -222,12 +226,13 @@
             low, weight, preferred_element_type=jnp.float32
         )
 
-    theirs, ours = rows_of(128 * (1 - core), 128), rows_of(128 * core, 128)
-    coef[...] = split_dot(field[theirs, :], right_w[...])
-    coef_sib = send(coef, in_core, sibling)
-    own_coef = split_dot(field[ours, :], right_w[...])
-    recv(coef_sib)
-    coef_core[...] = own_coef + in_core[...]
+    recv(to_core[0])
+    recv(right_sib)
+    settle(0)
+    early = split_dot(field[0], right_w[0])
+    recv(to_core[1])
+    settle(1)
+    coef_core[...] = early + split_dot(field[1], right_w[1])
     pair = lax.div(z_lo, 2)
     to_y = []
     for part in (1 - pair, pair):
@@ -283,23 +288,21 @@
     for copy in over:
         recv(copy)
     for o in range(4):
-        eight = rows_of(128 * core + 32 * y + 8 * lax.rem(z_lo + 4 - o, 4), 8)
+        eight = rows_of(32 * y + 8 * lax.rem(z_lo + 4 - o, 4), 8)
         beside = node[:, RANK:] if o == 0 else in_near[o]
         partner[eight, :RANK] = in_flip[o, :, :RANK]
         partner[eight, RANK:] = in_flip[o, :, RANK:] + beside
 
-    def thirty_two(y_):
-        return partner.at[rows_of(128 * core + 32 * y_, 32), :]
-
-    back = [send(thirty_two(y), thirty_two(y), at(y_=y_off(o))) for o in (2, 1, 3)]
-    relays = [send(thirty_two(y), thirty_two(y), at(y_=y_off(o), core_=1 - core)) for o in (2, 1, 3)]
-    relays.append(send(thirty_two(y), thirty_two(y), sibling))
+    thirty_two = partner.at[rows_of(32 * y, 32), :]
+    back = [send(thirty_two, thirty_two, at(y_=y_off(o))) for o in (2, 1, 3)]
+    recv(left_sib)
     for copy in back:
         recv(copy)
-    out_ref[ours, :] = field[ours, :] + split_dot(partner[ours, :], left_t[...])
-    for copy in relays:
-        recv(copy)
-    out_ref[theirs, :] = field[theirs, :] + split_dot(partner[theirs, :], left_t[...])
+    ours = rows_of(128 * core, 128)
+    out_far[...] = field[1 - core] + split_dot(partner[...], left_t[1 - core])
+    to_out = send(out_far, out_ref.at[ours, :], sibling)
+    out_ref[ours, :] = field[core] + split_dot(partner[...], left_t[core])
+    recv(to_out)
     for copy in copies:
         copy.wait_send()
 
@@ -311,17 +314,14 @@
         ((32, 128), jnp.int32),
         ((SLOTS, 128), jnp.int32),
         ((SLOTS, CASES), bf16),
-        ((ROWS, SLOTS), bf16),
-        ((ROWS, SLOTS), bf16),
+        ((2, ROWS, SLOTS), bf16),
         ((LEVELS, ROWS, RANK), bf16),
         ((LEVELS, ROWS, RANK), bf16),
-        ((WIDE, ROWS), bf16),
-        ((ROWS, WIDE), bf16),
-        ((ROWS, CASES), f32),
-        ((ROWS, CASES), f32),
-        ((CASES, ROWS), f32),
-        ((128, WIDE), f32),
-        ((128, WIDE), f32),
+        ((2, WIDE, ROWS), bf16),
+        ((2, ROWS, WIDE), bf16),
+        ((2, 2, ROWS, 128), f32),
+        ((2, ROWS, 128), f32),
+        ((2, 128, ROWS), f32),
         ((128, WIDE), f32),
         ((4, 32, WIDE), f32),
         ((32, WIDE), f32),
@@ -331,7 +331,8 @@
         ((4, 8, RANK), f32),
         ((4, 8, RANK), f32),
         ((4, 2, 8, RANK), f32),
-        ((CASES, WIDE), f32),
+        ((128, WIDE), f32),
+        ((128, ROWS), f32),
         ((RANK, WIDE), f32),
         ((64, WIDE), f32),
         ((64, WIDE), f32),

time: 53.8 us -> 52.3 us (0.972)
  Pallas kernels: 52.2 us -> 50.8 us
    pallas_call x1, Pallas kernels: 52.2 us -> 50.8 us  [body(): pl.pallas_call(kernel, out_shape=pltpu.VMEM((CASES, ROWS), f32), in_specs...]
where the time goes in v4:
time: 52.3 us
  Pallas kernels  50.8 us (97%)
  local copies, waits for them, and re-layouts  0.8 us (2%)
  between operations  0.66 us (1%)
    pallas_call x1, Pallas kernels, body(): pl.pallas_call(kernel, out_shape=pltpu.VMEM((CASES, ROWS), f32), in_specs...  50.8 us

profile of v4, /device:TPU:1, one launch (start us, length us, event | category | flops | bytes accessed | tf_op | source)
XLA Modules:
  0.0 52.3 jit_solution(16777609624967865690)
XLA Ops:
  0.7 50.8 %shard_map.64 = f32[256,512]{1,0:T(8,128)S(1)} custom-call(bf16[256,512]{1,0:T(8,128)(2,1)} %loads_ref.1, s32[1]{0:T(128)S(6)} %copy.9.size_ref, s32[32,128]{1,0:T(8,128)} %bitcast.1, bf16[512,4096]{1,0:T(8,128)(2,1)} %inverse_ref.1, bf16[3,512,128]{2,1,0:T(8,128)(2,1)} %left_ref.1, bf16[3,512,128]{2,1,0:T(8,128)(2,1)} %right_ref.1), custom_call_target="tpu_custom_call" | custom-call | tf_op jit(solution)/shard_map/pallas_call | solution.py:347
  51.5 0.8 %copy.8 = f32[256,512]{1,0:T(8,128)} copy(f32[256,512]{1,0:T(8,128)S(1)} %shard_map.64) | data formatting | bytes 1048576

commit v5 on v4

--- a/solution.py
+++ b/solution.py
@@ -188,24 +188,29 @@
 
     recv(forwards[0])
     recv(forwards[2])
-    permute([(2, 0, quarter), (2, 3 * quarter, quarter)])
     recv(forwards[1])
     recv(forwards[3])
-    permute([(2, quarter, HALF)])
+    permute([(2, 0, ROWS)])
 
     got_inverse.wait()
     recv(inverse_sib)
-    to_core = []
-
-    def solve(b, start, count):
-        rows = pl.ds(start, count)
-        solved = jnp.dot(inverse[b, rows, :], ordered[...], preferred_element_type=jnp.float32)
+    base = len(copies)
+
+    def swap(b):
+        return pltpu.make_async_remote_copy(
+            src_ref=partial.at[1 - core, b], dst_ref=from_core.at[b], send_sem=send_sem.at[base + b],
+            recv_sem=recv_sem.at[base + b], device_id=sibling, device_id_type=MESH,
+        )
+
+    @pl.loop(0, 2)
+    def _(b):
+        solved = jnp.dot(inverse[b], ordered[...], preferred_element_type=jnp.float32)
         for h in range(2):
-            partial[h, b, rows, :] = solved[:, 128 * h:128 * h + 128]
-        to_core.append(send(partial.at[1 - core, b, rows, :], from_core.at[b, rows, :], sibling))
-
-    solve(0, 0, ROWS)
-    solve(1, 0, ROWS)
+            partial[h, b] = solved[:, 128 * h:128 * h + 128]
+        swap(b).start()
+
+    to_core = [swap(0), swap(1)]
+    copies += to_core
     for copy in mix_across:
         recv(copy)
     mine = rows_of(64 * core + 16 * z_lo, 16)

time: 52.3 us -> 50.3 us (0.962)
  Pallas kernels: 50.8 us -> 48.8 us
    pallas_call x1, Pallas kernels: 50.8 us -> 48.8 us  [body(): pl.pallas_call(kernel, out_shape=pltpu.VMEM((CASES, ROWS), f32), in_specs...]
where the time goes in v5:
time: 50.3 us; the launch traced here: 50.2 us
  Pallas kernels  48.8 us (97%)
  local copies, waits for them, and re-layouts  0.8 us (2%)
  between operations  0.66 us (1%)
    pallas_call x1, Pallas kernels, body(): pl.pallas_call(kernel, out_shape=pltpu.VMEM((CASES, ROWS), f32), in_specs...  48.8 us

profile of v5, /device:TPU:1, one launch (start us, length us, event | category | flops | bytes accessed | tf_op | source)
XLA Modules:
  0.0 50.2 jit_solution(4417083830389811246)
XLA Ops:
  0.7 48.8 %shard_map.64 = f32[256,512]{1,0:T(8,128)S(1)} custom-call(bf16[256,512]{1,0:T(8,128)(2,1)} %loads_ref.1, s32[1]{0:T(128)S(6)} %copy.9.size_ref, s32[32,128]{1,0:T(8,128)} %bitcast.1, bf16[512,4096]{1,0:T(8,128)(2,1)} %inverse_ref.1, bf16[3,512,128]{2,1,0:T(8,128)(2,1)} %left_ref.1, bf16[3,512,128]{2,1,0:T(8,128)(2,1)} %right_ref.1), custom_call_target="tpu_custom_call" | custom-call | tf_op jit(solution)/shard_map/pallas_call | solution.py:352
  49.4 0.8 %copy.8 = f32[256,512]{1,0:T(8,128)} copy(f32[256,512]{1,0:T(8,128)S(1)} %shard_map.64) | data formatting | bytes 1048576

commit v6 on v5

--- a/solution.py
+++ b/solution.py
@@ -231,13 +231,15 @@
             low, weight, preferred_element_type=jnp.float32
         )
 
-    recv(to_core[0])
     recv(right_sib)
-    settle(0)
-    early = split_dot(field[0], right_w[0])
-    recv(to_core[1])
-    settle(1)
-    coef_core[...] = early + split_dot(field[1], right_w[1])
+    coef_core[...] = jnp.zeros((128, WIDE), jnp.float32)
+
+    @pl.loop(0, 2)
+    def _(b):
+        swap(b).wait_recv()
+        settle(b)
+        coef_core[...] += split_dot(field[b], right_w[b])
+
     pair = lax.div(z_lo, 2)
     to_y = []
     for part in (1 - pair, pair):

time: 50.3 us -> 50.4 us (level)
  no operation moved by 1% of the time
where the time goes in v6:
time: 50.4 us; the launch traced here: 50.3 us
  Pallas kernels  48.8 us (97%)
  local copies, waits for them, and re-layouts  0.8 us (2%)
  between operations  0.66 us (1%)
    pallas_call x1, Pallas kernels, body(): pl.pallas_call(kernel, out_shape=pltpu.VMEM((CASES, ROWS), f32), in_specs...  48.8 us

profile of v6, /device:TPU:1, one launch (start us, length us, event | category | flops | bytes accessed | tf_op | source)
XLA Modules:
  0.0 50.3 jit_solution(121696233323089845)
XLA Ops:
  0.7 48.8 %shard_map.64 = f32[256,512]{1,0:T(8,128)S(1)} custom-call(bf16[256,512]{1,0:T(8,128)(2,1)} %loads_ref.1, s32[1]{0:T(128)S(6)} %copy.9.size_ref, s32[32,128]{1,0:T(8,128)} %bitcast.1, bf16[512,4096]{1,0:T(8,128)(2,1)} %inverse_ref.1, bf16[3,512,128]{2,1,0:T(8,128)(2,1)} %left_ref.1, bf16[3,512,128]{2,1,0:T(8,128)(2,1)} %right_ref.1), custom_call_target="tpu_custom_call" | custom-call | tf_op jit(solution)/shard_map/pallas_call | solution.py:354
  49.5 0.8 %copy.8 = f32[256,512]{1,0:T(8,128)} copy(f32[256,512]{1,0:T(8,128)S(1)} %shard_map.64) | data formatting | bytes 1048576
